TPU v7x, 256 devices: a whole 4x4x8 slice. The times are simulated.
256 devices in a mesh: dp: 16 (over x, y_hi, core), mp: 16 (over y_lo, z).
Axes of the slice: x: 4, y: 4 (y_hi: 2, y_lo: 2; y = y_hi * 2 + y_lo), z: 8, core: 2. Of those that a mesh axis runs over, the one named last changes fastest.
Arguments:
- acts: bfloat16 [4096, 8, 2048], P('dp', None, 'mp'), may hold values from -6 to 6
- cotangent: bfloat16 [4096, 8, 1024], P('dp'), may hold values from -0.09375 to 0.09375
- block_slot: int32 [8], replicated, may hold values from 0 to 31, as said below
- basis_in: bfloat16 [32, 2048, 2048], P('dp', None, 'mp'), may hold values from -0.125 to 0.125
- basis_out: bfloat16 [32, 1024, 1024], P('dp', 'mp'), may hold values from -0.1875 to 0.1875
- moment_first: float32 [32, 2048, 1024], P('dp', 'mp'), may hold values from -3 to 3
- moment_second: float32 [32, 2048, 1024], P('dp', 'mp'), may hold values from 0.05 to 2
Outputs:
- new_first: float32 [32, 2048, 1024], P('dp', 'mp')
- new_second: float32 [32, 2048, 1024], P('dp', 'mp')
- stat_in: float32 [32, 2048, 2048], P('dp', 'mp')
- update: bfloat16 [8, 2048, 1024], P(None, 'mp', 'dp')
Inputs may be any that keep to these rules, and one draw needn't show every extreme that they name: `block_slot`: the values are distinct. Slot s belongs to preconditioner group s // 2; in every draw one group owns 2 blocks and every other group owns at most one.
All inputs are finite; a program needn't handle non-finite values.
Results may differ from a plain program's by a relative error of at most 0.03.
Values may be sent and summed in bfloat16 or wider, within the bound.
A program may use at most 128 MiB of HBM per device.

v0:
```python
import jax
import jax.numpy as jnp
from jax import lax
from jax.sharding import PartitionSpec as P


def per_device(acts, cotangent, block_slot, basis_in, basis_out, moment_first, moment_second):
    group_count = lax.axis_size("dp")
    slot_count = basis_in.shape[0]
    learner = jnp.einsum("tbr,tbo->bro", acts, cotangent, preferred_element_type=jnp.float32)
    slot_ids = jnp.arange(group_count * slot_count, dtype=jnp.int32)
    placing = (slot_ids[:, None] == block_slot[None, :]).astype(jnp.float32)
    totals = lax.psum(learner.astype(jnp.bfloat16), "dp").astype(jnp.float32)
    own_slots = lax.dynamic_slice_in_dim(placing, lax.axis_index("dp") * slot_count, slot_count, 0)
    summed = jnp.einsum("sb,bro->sro", own_slots, totals, precision=lax.Precision.HIGHEST)
    grad_block = summed.astype(jnp.bfloat16)
    block_piece = lax.all_gather(grad_block, "mp", axis=1, tiled=True)
    basis_piece = basis_in
    left_acc = jnp.einsum(
        "scr,sco->sro", basis_piece, block_piece, preferred_element_type=jnp.float32
    )
    stat_part = jnp.einsum(
        "sro,sco->src", grad_block, block_piece, preferred_element_type=jnp.float32
    )
    left_acc, stat_in = (left_acc, stat_part)
    left_rotated = left_acc.astype(jnp.bfloat16)
    full_basis = lax.all_gather(basis_out, "mp", axis=1, tiled=True)
    rotated = jnp.einsum(
        "srk,sko->sro", left_rotated, full_basis, preferred_element_type=jnp.float32
    )
    new_first = 0.9 * moment_first + 0.1 * rotated
    new_second = 0.95 * moment_second + 0.05 * rotated * rotated
    direction = (new_first / jnp.sqrt(new_second)).astype(jnp.bfloat16)
    back_full = jnp.einsum(
        "sro,sko->srk", direction, full_basis, preferred_element_type=jnp.float32
    )
    back_rotated = back_full.astype(jnp.bfloat16)
    basis_piece = basis_in
    update_rows = lax.psum_scatter(
        jnp.einsum(
            "scr,sro->cso", basis_piece, back_rotated, preferred_element_type=jnp.float32
        ).astype(jnp.bfloat16),
        "mp",
        scatter_dimension=0,
        tiled=True,
    )
    returned = lax.all_to_all(update_rows, "dp", split_axis=2, concat_axis=1, tiled=True)
    selected = jnp.take(returned, block_slot, axis=1)
    update = jnp.transpose(selected, (1, 0, 2))
    return (new_first, new_second, stat_in, update)


def solution(mesh):
    placed = (
        P("dp", None, "mp"),
        P("dp", None, None),
        P(),
        P("dp", None, "mp"),
        P("dp", "mp", None),
        P("dp", "mp", None),
        P("dp", "mp", None),
    )
    return jax.shard_map(
        per_device,
        mesh=mesh,
        in_specs=placed,
        out_specs=(
            P("dp", "mp", None),
            P("dp", "mp", None),
            P("dp", "mp", None),
            P(None, "mp", "dp"),
        ),
        check_vma=False,
    )
```

profile of v0, /device:TPU:1, one launch (start us, length us, event | category | flops | bytes accessed | tf_op | source)
XLA Modules:
  0.0 454.5 jit_solution(5039546534541447685)
XLA Ops:
  8.0 0.0 copy-start
  8.0 0.0 copy-start.4
  8.0 0.0 all-reduce.2.cloned.1.call-start
  8.1 8.6 %fusion.8 = bf16[8,128,1024]{2,1,0:T(8,128)(2,1)} fusion(bf16[256,8,1024]{2,1,0:T(8,128)(2,1)} %param.8, bf16[256,8,128]{2,1,0:T(8,128)(2,1)} %param.7), kind=kOutput, calls=%fused_computation.10 | convolution fusion | flops 537919488 | bytes 6815744 | tf_op jit(solution)/shard_map/tbr,tbo->bro/dot_general | solution.py:10
  16.7 0.0 all-reduce.2.cloned.1.call-update
  16.7 0.0 all-gather.5.cloned.1.call-start
  16.8 0.5 all-gather.5.cloned.1.call-update
  17.3 0.0 all-gather.3.cloned.1.call-start
  17.4 170.0 %all-reduce.2.cloned.1.call-done = bf16[8,128,1024]{2,1,0:T(8,128)(2,1)} async-done(((bf16[8,128,1024]{2,1,0:T(8,128)(2,1)}), bf16[8,128,1024]{2,1,0:T(8,128)(2,1)}) %all-reduce.2.cloned.1.call-update) | async-done | bytes 2097168 | tf_op jit(solution)/shard_map/psum | solution.py:13
  187.3 0.0 copy-done.4
  187.3 3.8 fusion.11
  191.1 0.0 all-gather.3.cloned.1.call-update
  191.2 0.2 reduce-scatter.4.cloned.1.call-start
  191.4 0.0 all-gather.5.cloned.1.call-done
  191.4 102.0 %all-gather.3.cloned.1.call-done = bf16[2,2048,1024]{2,0,1:T(2,128)(2,1)} async-done(((bf16[2,128,1024]{2,0,1:T(2,128)(2,1)}), bf16[2,2048,1024]{2,0,1:T(2,128)(2,1)}) %all-gather.3.cloned.1.call-update) | async-done | bytes 8388624 | tf_op jit(solution)/shard_map/all_gather | solution.py:17
  293.4 9.6 %fusion.20 = (f32[2,128,1024]{2,1,0:T(8,128)S(1)}, f32[2,128,1024]{2,1,0:T(8,128)S(1)}) fusion(f32[2,128,1024]{2,1,0:T(8,128)} %param.13, f32[2,128,1024]{2,1,0:T(8,128)} %param.12, bf16[2,1024,1024]{2,1,0:T(8,128)(2,1)} %all-gather.5.cloned.1.call-done, bf16[2,2048,128]{2,1,0:T(8,128)(2,1)S(1)} %copy-done, ...), kind=kOutput, calls=%fused_computation.16 | convolution fusion | flops 1612709888 | bytes 17825792 | tf_op jit(solution)/shard_map/srk,sko->sro/dot_general | solution.py:28
  303.1 0.0 copy-start.1
  303.1 0.0 copy-start.2
  303.1 10.2 %convolution_convert_fusion = bf16[2,1024,2048]{2,1,0:T(8,128)(2,1)} fusion(bf16[2,2048,128]{2,1,0:T(8,128)(2,1)S(1)} %copy-done, bf16[2,1024,1024]{2,1,0:T(8,128)(2,1)} %all-gather.5.cloned.1.call-done, f32[2,128,1024]{2,1,0:T(8,128)S(1)} %get-tuple-element.5, f32[2,128,1024]{2,1,0:T(8,128)S(1)} %get-tuple-element.4), kind=kOutput, calls=%fused_computation.5 | convolution fusion | flops 1615593472 | bytes 15728640 | tf_op jit(solution)/shard_map/scr,sro->cso/dot_general | solution.py:40
  313.3 0.0 copy-done.2
  313.3 12.3 %copy.40 = bf16[2048,2048]{1,0:T(8,128)(2,1)} copy(bf16[2048,2048]{0,1:T(8,128)(2,1)} %bitcast.16) | data formatting | bytes 16777216
  325.6 0.0 reduce-scatter.4.cloned.1.call-update
  325.6 98.9 %reduce-scatter.4.cloned.1.call-done = bf16[128,2048]{1,0:T(8,128)(2,1)} async-done(((bf16[2048,2048]{1,0:T(8,128)(2,1)}), bf16[128,2048]{1,0:T(8,128)(2,1)}) %reduce-scatter.4.cloned.1.call-update) | async-done | bytes 524304
  424.5 1.3 copy.41
  425.8 1.4 copy.33
  427.2 7.1 %all-to-all-start = ((bf16[128,2,1024]{0,1,2:T(2,128)(2,1)}), bf16[128,2,1024]{0,1,2:T(2,128)(2,1)S(1)}, u32[]{:S(2)}, u32[]{:S(2)}) async-start(bf16[128,2,1024]{0,1,2:T(2,128)(2,1)} %copy.33), calls=%async_computation | async-start | bytes 1048576 | tf_op jit(solution)/shard_map/all_to_all | solution.py:47
  434.3 0.0 copy-done.3
  434.3 7.8 %fusion.2 = f32[2,128,2048]{2,1,0:T(8,128)} fusion(bf16[2,2048,1024]{2,0,1:T(2,128)(2,1)} %all-gather.3.cloned.1.call-done, bf16[2,128,1024]{2,0,1:T(2,128)(2,1)S(1)} %copy-done.3), kind=kOutput, calls=%fused_computation.3 | convolution fusion | flops 1073741824 | bytes 11010048 | tf_op jit(solution)/shard_map/sro,sco->src/dot_general | solution.py:22
  442.1 3.3 all-to-all-done
  445.4 0.1 copy.34
  445.6 0.6 gather_fusion
  446.1 0.7 broadcast_select_fusion
  (7 shorter events, 0.1 us)
Async XLA Ops:
  8.0 285.4 %copy-start = (bf16[2,2048,128]{2,1,0:T(8,128)(2,1)S(1)}, bf16[2,2048,128]{2,1,0:T(8,128)(2,1)}, u32[]{:S(2)}) copy-start(bf16[2,2048,128]{2,1,0:T(8,128)(2,1)} %param.10) | copy-start | bytes 3145732
  8.0 179.3 %copy-start.4 = (s32[8]{0:T(128)S(1)}, s32[8]{0:T(128)}, u32[]{:S(2)}) copy-start(s32[8]{0:T(128)} %param.9) | copy-start | bytes 100
  8.0 179.3 %all-reduce.2.cloned.1.call-start = ((), (), s32[]{:S(2)}) async-start(), calls=%async_computation.2 | async-start | bytes 4194304 | tf_op jit(solution)/shard_map/psum | solution.py:13
  16.7 174.7 %all-gather.5.cloned.1.call-start = ((), (), s32[]{:S(2)}) async-start(), calls=%async_computation.4 | async-start | bytes 4456448 | tf_op jit(solution)/shard_map/all_gather | solution.py:27
  17.3 276.1 %all-gather.3.cloned.1.call-start = ((), (), s32[]{:S(2)}) async-start(), calls=%async_computation.3 | async-start | bytes 8912896 | tf_op jit(solution)/shard_map/all_gather | solution.py:17
  191.2 233.3 %reduce-scatter.4.cloned.1.call-start = ((), (), s32[]{:S(2)}) async-start(), calls=%async_computation.5 | async-start | bytes 8912896
  303.1 10.2 %copy-start.1 = (f32[2,128,1024]{2,1,0:T(8,128)}, f32[2,128,1024]{2,1,0:T(8,128)S(1)}, u32[]{:S(2)}) copy-start(f32[2,128,1024]{2,1,0:T(8,128)S(1)} %get-tuple-element.4) | copy-start | bytes 3145732
  303.1 10.2 %copy-start.2 = (f32[2,128,1024]{2,1,0:T(8,128)}, f32[2,128,1024]{2,1,0:T(8,128)S(1)}, u32[]{:S(2)}) copy-start(f32[2,128,1024]{2,1,0:T(8,128)S(1)} %get-tuple-element.5) | copy-start | bytes 3145732
  325.6 108.8 %copy-start.3 = (bf16[2,128,1024]{2,0,1:T(2,128)(2,1)S(1)}, bf16[2,128,1024]{2,0,1:T(2,128)(2,1)}, u32[]{:S(2)}) copy-start(bf16[2,128,1024]{2,0,1:T(2,128)(2,1)} %fusion.11) | copy-start | bytes 1572868
  427.2 18.3 %all-to-all-start = ((bf16[128,2,1024]{0,1,2:T(2,128)(2,1)}), bf16[128,2,1024]{0,1,2:T(2,128)(2,1)S(1)}, u32[]{:S(2)}, u32[]{:S(2)}) async-start(bf16[128,2,1024]{0,1,2:T(2,128)(2,1)} %copy.33), calls=%async_computation | async-start | bytes 1048576 | tf_op jit(solution)/shard_map/all_to_all | solution.py:47
Sparse Core Ops, SparseCore 0:
  16.9 170.4 all-reduce.1
Sparse Core Ops, SparseCore 1:
  19.0 72.6 all-gather.4
  191.2 102.1 all-gather.2
  325.7 98.8 reduce-scatter.3
where the time goes:
time: 455 us; the launch traced here: 454 us
  waiting for transfers between devices  375 us (82%)
  matrix products  40.1 us (9%)
  between operations  15.8 us (3%)
  local copies, waits for them, and re-layouts  15.6 us (3%)
  starting transfers between devices  7.48 us (2%)
    psum x1, waiting for transfers between devices, per_device(): totals = lax.psum(learner.astype(jnp.bfloat16), 'dp').astype(jnp.float32)  170 us
    all_gather x1, waiting for transfers between devices, per_device(): block_piece = lax.all_gather(grad_block, 'mp', axis=1, tiled=True)  102 us
    unnamed x5, waiting for transfers between devices  99.4 us
    unnamed x12, local copies, waits for them, and re-layouts  13.6 us
    dot_general x1, matrix products, per_device(): jnp.einsum('scr,sro->cso', basis_piece, back_rotated, preferred_element_t...  10.2 us
    dot_general x1, matrix products, per_device(): jnp.einsum('srk,sko->sro', left_rotated, full_basis, preferred_element_ty...  9.64 us
  transfers between devices with their start and end apart: 5, of which 4 were waited for; matrix products, arithmetic and copies ran while one was open for 3% of the time, Pallas kernels for 0%

commit v1 on v0

v1 whole, which is shorter than its diff:
```python
import functools

import jax
import jax.numpy as jnp
from jax import lax
from jax.experimental import pallas as pl
from jax.experimental.pallas import tpu as pltpu
from jax.sharding import PartitionSpec as P

MESH = pl.DeviceIdType.MESH
BF = jnp.bfloat16
F32 = jnp.float32
NX, NZ = 4, 8
NB = 8


def nt(a, b):
    return lax.dot_general(a, b, (((1,), (1,)), ((), ())), preferred_element_type=F32)


def nn(a, b):
    return jnp.dot(a, b, preferred_element_type=F32)


def tn(a, b):
    return lax.dot_general(a, b, (((0,), (0,)), ((), ())), preferred_element_type=F32)


class Net:
    def __init__(self, ssem, rsem):
        self.ssem, self.rsem, self.used, self.sent = ssem, rsem, 0, []
        dp, mp = lax.axis_index("dp"), lax.axis_index("mp")
        self.x, self.yh, self.c = dp // 4, (dp // 2) % 2, dp % 2
        self.yl, self.z = mp // NZ, mp % NZ

    def at(self, x=None, yh=None, c=None, yl=None, z=None):
        x = self.x if x is None else x
        yh = self.yh if yh is None else yh
        c = self.c if c is None else c
        yl = self.yl if yl is None else yl
        z = self.z if z is None else z
        return (x * 4 + yh * 2 + c, yl * NZ + z)

    def send(self, src, dst, device):
        i = self.used
        self.used += 1
        copy = pltpu.make_async_remote_copy(
            src_ref=src,
            dst_ref=dst,
            send_sem=self.ssem.at[i],
            recv_sem=self.rsem.at[i],
            device_id=device,
            device_id_type=MESH,
        )
        copy.start()
        self.sent.append(copy)
        return copy

    def drain(self):
        for copy in self.sent:
            copy.wait_send()

    def mate(self, src, dst):
        return self.send(src, dst, self.at(c=1 - self.c))

    def xs(self):
        return [lax.rem(self.x + k, NX) for k in (1, 2, 3)]


class Scatter:
    def __init__(self, net, t, bufs, out, kind, step):
        self.net, self.t, self.out, self.kind, self.step = net, t, out, kind, step
        self.x0, self.y0, self.y1, self.x1 = bufs
        self.rows = t.shape[2]
        self.half = self.rows // 2

    def start(self):
        net, h = self.net, self.half
        self.cy1 = net.send(
            self.t.at[:, 1 - net.yh, pl.ds(h, h), :], self.y1, net.at(yh=1 - net.yh)
        )
        self.cx0 = [
            net.send(self.t.at[xp, :, pl.ds(0, h), :], self.x0.at[k], net.at(x=xp))
            for k, xp in enumerate(net.xs())
        ]

    def add(self, dst, srcs):
        total = None
        n, kind = self.step, self.kind

        def body(i, carry):
            rows = pl.ds(pl.multiple_of(i * n, n), n)
            total = None
            for src in srcs:
                part = src(rows).astype(kind)
                total = part if total is None else total + part
            dst(rows, total.astype(BF))
            return carry

        del total
        lax.fori_loop(0, self.half // n, body, 0)

    def rows_of(self, ref, base=0):
        def load(rows):
            return ref[pl.ds(pl.multiple_of(rows.start + base, 16), rows.size), :]

        return load

    def store_of(self, ref, base=0):
        def store(rows, value):
            ref[pl.ds(pl.multiple_of(rows.start + base, 16), rows.size), :] = value

        return store

    def middle(self):
        net, h, t = self.net, self.half, self.t
        for copy in self.cx0:
            copy.wait_recv()
        for yp in (1 - net.yh, net.yh):
            mine = t.at[net.x, yp]
            self.add(
                self.store_of(mine),
                [self.rows_of(mine)] + [self.rows_of(self.x0.at[k, yp]) for k in range(3)],
            )
            if yp is not net.yh:
                self.cy0 = net.send(
                    t.at[net.x, 1 - net.yh, pl.ds(0, h), :], self.y0, net.at(yh=1 - net.yh)
                )
        self.cy1.wait_recv()
        self.cx1 = []
        for k, xp in enumerate(net.xs() + [net.x]):
            mine = t.at[xp, net.yh]
            self.add(self.store_of(mine, h), [self.rows_of(mine, h), self.rows_of(self.y1.at[xp])])
            if k < 3:
                self.cx1.append(
                    net.send(t.at[xp, net.yh, pl.ds(h, h), :], self.x1.at[k], net.at(x=xp))
                )

    def finish(self):
        net, h = self.net, self.half
        mine = self.t.at[net.x, net.yh]
        self.cy0.wait_recv()
        self.add(self.store_of(self.out), [self.rows_of(mine), self.rows_of(self.y0)])
        for copy in self.cx1:
            copy.wait_recv()
        self.add(
            self.store_of(self.out, h),
            [self.rows_of(mine, h)] + [self.rows_of(self.x1.at[k]) for k in range(3)],
        )


class Spread:
    def __init__(self, net, a):
        self.net, self.a, self.half = net, a, a.shape[2] // 2

    def start(self):
        net, h, a = self.net, self.half, self.a
        last = a.at[net.x, net.yh, pl.ds(h, h), :]
        self.cy = net.send(last, last, net.at(yh=1 - net.yh))
        first = a.at[net.x, net.yh, pl.ds(0, h), :]
        self.cx = [net.send(first, first, net.at(x=xp)) for xp in net.xs()]

    def middle(self):
        net, h, a = self.net, self.half, self.a
        self.cy.wait_recv()
        last = a.at[net.x, :, pl.ds(h, h), :]
        self.cx2 = [net.send(last, last, net.at(x=xp)) for xp in net.xs()]
        for copy in self.cx:
            copy.wait_recv()
        first = a.at[:, net.yh, pl.ds(0, h), :]
        self.cy2 = net.send(first, first, net.at(yh=1 - net.yh))

    def finish(self):
        for copy in self.cx2:
            copy.wait_recv()
        self.cy2.wait_recv()


class Ring:
    def __init__(self, net, block):
        self.net, self.block = net, block
        self.up, self.down = {}, {}

    def hop(self, way, step, line):
        net = self.net
        yl = net.yl if line == 0 else 1 - net.yl
        sign = 1 if way == 0 else -1
        ref = self.block(yl, lax.rem(net.z - sign * step + NZ, NZ))
        copy = net.send(ref, ref, net.at(z=lax.rem(net.z + sign + NZ, NZ)))
        (self.up if way == 0 else self.down)[step, line] = copy

    def start(self):
        net = self.net
        own = self.block(net.yl, net.z)
        self.hop(0, 0, 0)
        self.hop(1, 0, 0)
        self.cy = net.send(own, own, net.at(yl=1 - net.yl))

    def step(self, s):
        if s == 0:
            self.cy.wait_recv()
            self.hop(0, 0, 1)
            self.hop(1, 0, 1)
            return
        for line in (0, 1):
            self.up[s - 1, line].wait_recv()
            if s < 3 or line == 0:
                self.hop(0, s, line)
            self.down[s - 1, line].wait_recv()
            if s < 3 or line == 1:
                self.hop(1, s, line)

    def finish(self):
        self.up[3, 0].wait_recv()
        self.down[3, 1].wait_recv()


def kernel(
    slot_ref, p_ref, b_ref, o_ref, m1_ref, m2_ref, r_out, s_out, u_out,
    prec, tg, gx0, gy0, gy1, gx1,
    cb, tb, bx0, by0, by1, bx1, bfull,
    co, to, ox0, oy0, oy1, ox1, ofin, oall,
    mb, cm, tm, mx0, my0, my1, mx1, mfin,
    gall, lfull, lacc, stat, smate, dfull, kbuf,
    rall, rpick, rmate, sall, spick, sgot,
    usend, urecv, ylsend, ylrecv, ufin, uall,
    ssem, rsem, asend, arecv,
):
    net = Net(ssem, rsem)
    x, yh, c, yl, z = net.x, net.yh, net.c, net.yl, net.z
    dp = lax.axis_index("dp")
    home = x * 2 + yh
    oc = 1 - c

    barrier = pltpu.get_barrier_semaphore()
    others = [
        net.at(x=lax.rem(x + i, NX), yh=lax.rem(yh + j, 2), c=lax.rem(c + k, 2))
        for i in range(4) for j in range(2) for k in range(2) if (i, j, k) != (0, 0, 0)
    ]
    others += [net.at(yl=1 - yl), net.at(z=lax.rem(z + 1, NZ)), net.at(z=lax.rem(z + NZ - 1, NZ))]
    for device in others:
        pl.semaphore_signal(barrier, inc=1, device_id=device, device_id_type=MESH)

    def pick(b):
        local = slot_ref[b] - (dp - c) * 2
        inside = (local >= 0) & (local < 4)
        return jnp.where(inside, lax.rem(local + 2 * c + 4, 4), 4)

    def block_of(group, s):
        found = 8
        for b in range(NB):
            found = jnp.where(slot_ref[b] == group * 2 + s, b, found)
        return found

    half_lanes = pl.ds(pl.multiple_of(c * 512, 512), 512)
    other_lanes = pl.ds(pl.multiple_of(oc * 512, 512), 512)
    half_b = pl.ds(pl.multiple_of(c * 1024, 1024), 1024)
    other_b = pl.ds(pl.multiple_of(oc * 1024, 1024), 1024)
    half_o = pl.ds(pl.multiple_of(c * 32, 32), 32)
    other_o = pl.ds(pl.multiple_of(oc * 32, 32), 32)

    for s in range(2):
        mb[s, 0:128, :] = m1_ref[s].astype(BF)
        mb[s, 128:256, :] = m2_ref[s].astype(BF)
    pl.semaphore_wait(barrier, len(others))

    pcopies = [
        net.mate(p_ref.at[pl.ds(i * 4, 4), :, other_lanes], prec.at[pl.ds(i * 4, 4)]) for i in range(2)
    ]
    bcopy = net.mate(b_ref.at[:, other_b, :], cb.at[pl.ds(2, 2)])
    ocopy = net.mate(o_ref.at[:, other_o, :], co.at[pl.ds(2, 2)])
    mcopy = net.mate(mb.at[:, :, other_lanes], cm.at[pl.ds(2, 2)])

    for i in range(2):
        pcopies[i].wait_recv()

        def add_cores(b, carry):
            total = p_ref[b, :, half_lanes].astype(F32) + prec[b].astype(F32)
            tg[b // 2, b % 2] = total.astype(BF)
            return carry

        lax.fori_loop(i * 4, i * 4 + 4, add_cores, 0)
    grads = Scatter(net, tg, (gx0, gy0, gy1, gx1), gall.at[yl, z], F32, 32)
    grads.start()

    for s in range(2):
        cb[s] = b_ref[s, half_b, :]
        co[s] = o_ref[s, half_o, :]
        cm[s] = mb[s, :, half_lanes]
    cb[4] = jnp.zeros_like(cb[4])
    co[4] = jnp.zeros_like(co[4])
    cm[4] = jnp.zeros_like(cm[4])
    bcopy.wait_recv()
    ocopy.wait_recv()
    mcopy.wait_recv()

    def choose(b, carry):
        i = pick(b)
        tb[b // 2, b % 2] = cb[i]
        to[b // 2, b % 2] = co[i]
        tm[b // 2, b % 2] = cm[i]
        return carry

    lax.fori_loop(0, NB, choose, 0)

    grads.middle()
    half16 = pl.ds(pl.multiple_of(c * 8, 8), 8)
    left = Scatter(net, tb, (bx0, by0, by1, bx1), None, BF, 128)
    right = Scatter(net, to, (ox0, oy0, oy1, ox1), oall.at[yl, z, c], BF, 16)
    moments = Scatter(net, tm, (mx0, my0, my1, mx1), mfin, BF, 32)
    left.out = bfull.at[half_b]
    left.start()
    right.start()
    grads.finish()

    gring = Ring(net, lambda a, b: gall.at[a, b])
    gring.start()
    gring.step(0)
    gring.step(1)
    left.middle()
    gring.step(2)
    right.middle()
    moments.start()
    gring.step(3)
    left.finish()
    bmate = net.mate(bfull.at[half_b], bfull.at[half_b])
    right.finish()
    oring = Ring(net, lambda a, b: oall.at[a, b, c])
    oring.start()
    oring.step(0)
    gring.finish()
    bmate.wait_recv()

    lacc[...] = jnp.zeros_like(lacc)
    mine = gall.at[yl, z]

    def rows_step(i, carry):
        part = gall[i // NZ, i % NZ]
        at = pl.multiple_of(i * 128, 128)
        lacc[...] += tn(bfull[pl.ds(at, 128), :], part)
        stat[:, pl.ds(at, 128)] = nt(mine[...], part)
        return carry

    lax.fori_loop(0, 16, rows_step, 0)
    lfull[:, half_lanes] = lacc[...].astype(BF)
    lmate = net.mate(lfull.at[:, half_lanes], lfull.at[:, half_lanes])
    mine_s = pl.ds(pl.multiple_of(c * 64, 64), 64)
    other_s = pl.ds(pl.multiple_of(oc * 64, 64), 64)
    cstat = net.mate(stat.at[other_s, :], smate)

    oring.step(1)
    moments.middle()
    oring.step(2)
    oring.step(3)
    oring.finish()
    omate = net.mate(oall.at[:, :, c], oall.at[:, :, c])
    cstat.wait_recv()
    sall[x, yh] = (stat[mine_s, :] + smate[...]).astype(BF)
    lmate.wait_recv()
    omate.wait_recv()

    basis = oall[:, :, :, :, half_lanes].reshape(1024, 512)
    rotated = nn(lfull[...], basis)
    rall[x, yh] = rotated.astype(BF)
    moments.finish()
    rspread = Spread(net, rall)
    rspread.start()
    first = 0.9 * mfin[0:128, :].astype(F32) + 0.1 * rotated
    second = 0.95 * mfin[128:256, :].astype(F32) + 0.05 * rotated * rotated
    dfull[:, half_lanes] = (first / jnp.sqrt(second)).astype(BF)
    dmate = net.mate(dfull.at[:, half_lanes], dfull.at[:, half_lanes])
    dmate.wait_recv()
    kbuf[...] = nt(dfull[...], oall[c].reshape(512, 1024)).astype(BF)

    sspread = Spread(net, sall)
    sspread.start()

    def part(zd, yd):
        at = pl.multiple_of((yd * NZ + zd) * 128, 128)
        return nn(bfull[pl.ds(at, 128), :], kbuf[...])

    hops = {}

    def ring_hop(way, s, yd):
        sign = 1 if way == 0 else -1
        value = part(lax.rem(z + sign * (4 - s) + NZ, NZ), yd)
        if (way, s - 1, yd) in hops:
            hops[way, s - 1, yd].wait_recv()
            value = value + urecv[way, s - 1, yd].astype(F32)
        usend[way, s, yd] = value.astype(BF)
        hops[way, s, yd] = net.send(
            usend.at[way, s, yd], urecv.at[way, s, yd], net.at(z=lax.rem(z + sign + NZ, NZ))
        )

    def ring_step(s):
        for yd in (0, 1):
            for way in (0, 1):
                if s > 0 or way == yd:
                    ring_hop(way, s, yd)

    ring_step(0)
    ring_step(1)
    rspread.middle()
    ring_step(2)
    sspread.middle()
    ring_step(3)

    rspread.finish()
    zero_r = jnp.zeros((128, 512), BF)
    zero_s = jnp.zeros((64, 2048), BF)

    def chosen(ref, zero, group, s):
        b = block_of(group, s)
        b0 = jnp.minimum(b, NB - 1)
        return jnp.where(b < NB, ref[b0 // 2, b0 % 2], zero)

    mate_group = dp - c + oc
    for s in range(2):
        rpick[s] = chosen(rall, zero_r, mate_group, s)
    crm = net.mate(rpick, rmate)

    for way in (0, 1):
        for yd in (0, 1):
            hops[way, 3, yd].wait_recv()

    def final(yd):
        return part(z, yd) + urecv[0, 3, yd].astype(F32) + urecv[1, 3, yd].astype(F32)

    ylsend[...] = final(1 - yl).astype(BF)
    cyl = net.send(ylsend, ylrecv, net.at(yl=1 - yl))
    own = final(yl)
    sspread.finish()
    for s in range(2):
        spick[s] = chosen(sall, zero_s, mate_group, s)
    csm = net.mate(spick, sgot)
    cyl.wait_recv()
    ufin[...] = (own + ylrecv[...].astype(F32)).astype(BF)

    def to_columns(j, k):
        tx, ty = 2 * c + j // 2, j % 2
        here = (tx == x) & (ty == yh) & (k == c)
        src = ufin.at[:, pl.ds(j * 128, 128)]

        def copy():
            return pltpu.make_async_remote_copy(
                src_ref=src,
                dst_ref=uall.at[home],
                send_sem=asend.at[j * 2 + k],
                recv_sem=arecv.at[home],
                device_id=net.at(x=tx, yh=ty, c=k),
                device_id_type=MESH,
            )

        return here, copy

    for j in range(4):
        for k in range(2):
            here, copy = to_columns(j, k)

            @pl.when(jnp.logical_not(here))
            def _(copy=copy):
                copy().start()

            @pl.when(here)
            def _(j=j):
                uall[home] = ufin[:, j * 128 : (j + 1) * 128]

    for s in range(2):
        r_out[s, :, half_lanes] = chosen(rall, zero_r, dp, s)
        s_out[s, mine_s, :] = chosen(sall, zero_s, dp, s)
    crm.wait_recv()
    csm.wait_recv()
    for s in range(2):
        r_out[s, :, other_lanes] = rmate[s]
        s_out[s, other_s, :] = sgot[s]

    for b in range(NB):

        @pl.when(jnp.logical_not((b == home) & (c == x // 2)))
        def _(b=b):
            pltpu.make_async_remote_copy(
                src_ref=uall.at[b],
                dst_ref=uall.at[b],
                send_sem=asend.at[0],
                recv_sem=arecv.at[b],
                device_id=net.at(c=oc),
                device_id_type=MESH,
            ).wait_recv()

        value = uall[b]
        u_out[b] = jnp.where(c == 0, value[:, 0:64], value[:, 64:128])

    net.drain()
    for j in range(4):
        for k in range(2):
            here, copy = to_columns(j, k)

            @pl.when(jnp.logical_not(here))
            def _(copy=copy):
                copy().wait_send()


def scatter_bufs(rows, lanes):
    h = rows // 2
    return [
        pltpu.VMEM((4, 2, rows, lanes), BF),
        pltpu.VMEM((3, 2, h, lanes), BF),
        pltpu.VMEM((h, lanes), BF),
        pltpu.VMEM((4, h, lanes), BF),
        pltpu.VMEM((3, h, lanes), BF),
    ]


def step(block_slot, learner, basis_in, basis_out, moment_first, moment_second):
    vmem = pl.BlockSpec(memory_space=pltpu.VMEM)
    scratch = (
        [pltpu.VMEM((8, 128, 512), BF)] + scatter_bufs(128, 512)
        + [pltpu.VMEM((5, 1024, 128), BF)] + scatter_bufs(1024, 128) + [pltpu.VMEM((2048, 128), BF)]
        + [pltpu.VMEM((5, 32, 1024), BF)] + scatter_bufs(32, 1024)
        + [pltpu.VMEM((8, 128), BF), pltpu.VMEM((2, 8, 2, 32, 1024), BF)]
        + [pltpu.VMEM((2, 256, 1024), BF), pltpu.VMEM((5, 256, 512), BF)] + scatter_bufs(256, 512)
        + [pltpu.VMEM((256, 512), BF)]
        + [
            pltpu.VMEM((2, 8, 128, 512), BF),
            pltpu.VMEM((128, 1024), BF),
            pltpu.VMEM((128, 512), F32),
            pltpu.VMEM((128, 2048), F32),
            pltpu.VMEM((64, 2048), F32),
            pltpu.VMEM((128, 1024), BF),
            pltpu.VMEM((128, 512), BF),
            pltpu.VMEM((4, 2, 128, 512), BF),
            pltpu.VMEM((2, 128, 512), BF),
            pltpu.VMEM((2, 128, 512), BF),
            pltpu.VMEM((4, 2, 64, 2048), BF),
            pltpu.VMEM((2, 64, 2048), BF),
            pltpu.VMEM((2, 64, 2048), BF),
            pltpu.VMEM((2, 4, 2, 128, 512), BF),
            pltpu.VMEM((2, 4, 2, 128, 512), BF),
            pltpu.VMEM((128, 512), BF),
            pltpu.VMEM((128, 512), BF),
            pltpu.VMEM((128, 512), BF),
            pltpu.VMEM((8, 128, 128), BF),
            pltpu.SemaphoreType.DMA((128,)),
            pltpu.SemaphoreType.DMA((128,)),
            pltpu.SemaphoreType.DMA((8,)),
            pltpu.SemaphoreType.DMA((8,)),
        ]
    )
    return pl.pallas_call(
        kernel,
        out_shape=(
            jax.ShapeDtypeStruct((2, 128, 1024), BF),
            jax.ShapeDtypeStruct((2, 128, 2048), BF),
            jax.ShapeDtypeStruct((8, 128, 64), BF),
        ),
        in_specs=[pl.BlockSpec(memory_space=pltpu.SMEM)] + [vmem] * 5,
        out_specs=(vmem, vmem, vmem),
        scratch_shapes=scratch,
        compiler_params=pltpu.CompilerParams(
            collective_id=0, has_side_effects=True, vmem_limit_bytes=56 << 20
        ),
        name="soap_step",
    )(block_slot, learner, basis_in, basis_out, moment_first, moment_second)


def per_device(acts, cotangent, block_slot, basis_in, basis_out, moment_first, moment_second):
    learner = jnp.einsum("tbr,tbo->bro", acts, cotangent, preferred_element_type=F32).astype(BF)
    rotated, stat, update = step(block_slot, learner, basis_in, basis_out, moment_first, moment_second)
    rotated = rotated.astype(F32)
    new_first = 0.9 * moment_first + 0.1 * rotated
    new_second = 0.95 * moment_second + 0.05 * rotated * rotated
    return (new_first, new_second, stat.astype(F32), update)


def solution(mesh):
    placed = (
        P("dp", None, "mp"),
        P("dp", None, None),
        P(),
        P("dp", None, "mp"),
        P("dp", "mp", None),
        P("dp", "mp", None),
        P("dp", "mp", None),
    )
    return jax.shard_map(
        per_device,
        mesh=mesh,
        in_specs=placed,
        out_specs=(
            P("dp", "mp", None),
            P("dp", "mp", None),
            P("dp", "mp", None),
            P(None, "mp", "dp"),
        ),
        check_vma=False,
    )
```

time: 455 us -> 144 us (0.32)
  waiting for transfers between devices: 375 us -> 0 us
  Pallas kernels: 0 us -> 129 us
  matrix products: 40.1 us -> 8.57 us
  between operations: 15.8 us -> 0.65 us
  local copies, waits for them, and re-layouts: 15.6 us -> 1.83 us
  starting transfers between devices: 7.48 us -> 0 us
    psum x1 -> x0, waiting for transfers between devices: 170 us -> none  [per_device(): totals = lax.psum(learner.astype(jnp.bfloat16), 'dp').astype(jnp.float32)]
    pallas_call x0 -> x1, Pallas kernels: none -> 129 us  [step(): pl.pallas_call(kernel, out_shape=(jax.ShapeDtypeStruct((2, 128, 1024), BF...]
    all_gather x2 -> x0, waiting for transfers between devices: 102 us -> none  [the longest x1 102 us: per_device(): block_piece = lax.all_gather(grad_block, 'mp', axis=1, tiled=True)]
    unnamed x5 -> x0, waiting for transfers between devices: 99.4 us -> none
    dot_general x5 -> x1, matrix products: 40.1 us -> 8.57 us  [per_device(): jnp.einsum('tbr,tbo->bro', acts, cotangent, preferred_element_type=F32)]
    unnamed x12 -> x7, local copies, waits for them, and re-layouts: 13.6 us -> 1.83 us
    all_to_all x1 -> x0, starting transfers between devices: 7.14 us -> none  [per_device(): lax.all_to_all(update_rows, 'dp', split_axis=2, concat_axis=1, tiled=True)]
  transfers between devices with their start and end apart: 5 -> 0, of which waited for: 4 -> 0; matrix products, arithmetic and copies ran while one was open for 3% -> 0% of each run, Pallas kernels for 0% -> 0%
where the time goes in v1:
time: 144 us
  Pallas kernels  129 us (90%)
  matrix products  8.57 us (6%)
  other arithmetic  4.24 us (3%)
  local copies, waits for them, and re-layouts  1.83 us (1%)
    pallas_call x1, Pallas kernels, step(): pl.pallas_call(kernel, out_shape=(jax.ShapeDtypeStruct((2, 128, 1024), BF...  129 us
    dot_general x1, matrix products, per_device(): jnp.einsum('tbr,tbo->bro', acts, cotangent, preferred_element_type=F32)  8.57 us

profile of v1, /device:TPU:1, one launch (start us, length us, event | category | flops | bytes accessed | tf_op | source)
XLA Modules:
  0.0 144.2 jit_solution(10203114697112430992)
XLA Ops:
  0.6 8.6 %fusion.2.p_ref = bf16[8,128,1024]{2,1,0:T(8,128)(2,1)} fusion(bf16[256,8,1024]{2,1,0:T(8,128)(2,1)} %param.8, bf16[256,8,128]{2,1,0:T(8,128)(2,1)} %param.7), kind=kOutput, calls=%fused_computation.2 | convolution fusion | flops 537919488 | bytes 6815744 | tf_op jit(solution)/shard_map/tbr,tbo->bro/dot_general | solution.py:567
  9.2 0.0 copy-start
  9.2 0.0 copy-start.1
  9.2 128.9 %soap_step.1 = (bf16[2,128,1024]{2,1,0:T(8,128)(2,1)}, bf16[2,128,2048]{2,1,0:T(8,128)(2,1)}, bf16[8,128,64]{2,1,0:T(8,128)(2,1)}) custom-call(s32[8]{0:T(128)} %slot_ref.1, bf16[8,128,1024]{2,1,0:T(8,128)(2,1)} %fusion.2.p_ref, bf16[2,2048,128]{2,1,0:T(8,128)(2,1)} %b_ref.1, bf16[2,64,1024]{2,1,0:T(8,128)(2,1)} %o_ref.1, f32[2,128,1024]{2,1,0:T(8,128)} %m1_ref.1, ...), custom_call_target="tpu_custom_call" | custom-call | tf_op jit(solution)/shard_map/soap_step/pallas_call | solution.py:549
  138.1 0.0 copy-start.2
  138.1 1.8 %copy.13 = bf16[8,128,64]{1,2,0:T(8,128)(2,1)} copy(bf16[8,128,64]{2,1,0:T(8,128)(2,1)} %get-tuple-element.13) | data formatting | bytes 262144
  139.9 0.0 copy-done
  139.9 0.0 copy-done.1
  139.9 2.7 %fusion.6 = (f32[2,128,1024]{2,1,0:T(8,128)}, f32[2,128,1024]{2,1,0:T(8,128)}) fusion(bf16[2,128,1024]{2,1,0:T(8,128)(2,1)} %get-tuple-element.7, f32[2,128,1024]{2,1,0:T(8,128)S(1)} %copy-done.1, f32[2,128,1024]{2,1,0:T(8,128)S(1)} %copy-done), kind=kLoop, calls=%fused_computation.6 | loop fusion | flops 2097152 | bytes 4718592 | tf_op jit(solution)/shard_map/add | solution.py:571
  142.6 0.0 copy-done.2
  142.6 1.6 %convert_element_type.11 = f32[2,128,2048]{2,1,0:T(8,128)} convert(bf16[2,128,2048]{2,1,0:T(8,128)(2,1)S(1)} %copy-done.2) | non-fusion elementwise | flops 524288 | bytes 3145728 | tf_op jit(solution)/shard_map/convert_element_type | solution.py:572
Async XLA Ops:
  9.2 130.7 %copy-start = (f32[2,128,1024]{2,1,0:T(8,128)S(1)}, f32[2,128,1024]{2,1,0:T(8,128)}, u32[]{:S(2)}) copy-start(f32[2,128,1024]{2,1,0:T(8,128)} %m1_ref.1) | copy-start | bytes 3145732
  9.2 130.7 %copy-start.1 = (f32[2,128,1024]{2,1,0:T(8,128)S(1)}, f32[2,128,1024]{2,1,0:T(8,128)}, u32[]{:S(2)}) copy-start(f32[2,128,1024]{2,1,0:T(8,128)} %m2_ref.1) | copy-start | bytes 3145732
  138.1 4.5 %copy-start.2 = (bf16[2,128,2048]{2,1,0:T(8,128)(2,1)S(1)}, bf16[2,128,2048]{2,1,0:T(8,128)(2,1)}, u32[]{:S(2)}) copy-start(bf16[2,128,2048]{2,1,0:T(8,128)(2,1)} %get-tuple-element.8) | copy-start | bytes 3145732

commit v2 on v1

--- a/solution.py
+++ b/solution.py
@@ -74,15 +74,22 @@
         self.rows = t.shape[2]
         self.half = self.rows // 2
 
-    def start(self):
+    def start_x(self):
+        net, h = self.net, self.half
+        self.cx0 = [
+            net.send(self.t.at[xp, :, pl.ds(0, h), :], self.x0.at[k], net.at(x=xp))
+            for k, xp in enumerate(net.xs())
+        ]
+
+    def start_y(self):
         net, h = self.net, self.half
         self.cy1 = net.send(
             self.t.at[:, 1 - net.yh, pl.ds(h, h), :], self.y1, net.at(yh=1 - net.yh)
         )
-        self.cx0 = [
-            net.send(self.t.at[xp, :, pl.ds(0, h), :], self.x0.at[k], net.at(x=xp))
-            for k, xp in enumerate(net.xs())
-        ]
+
+    def start(self):
+        self.start_y()
+        self.start_x()
 
     def add(self, dst, srcs):
         total = None
@@ -177,8 +184,8 @@
 
 
 class Ring:
-    def __init__(self, net, block):
-        self.net, self.block = net, block
+    def __init__(self, net, block, seen):
+        self.net, self.block, self.seen = net, block, seen
         self.up, self.down = {}, {}
 
     def hop(self, way, step, line):
@@ -195,36 +202,51 @@
         self.hop(0, 0, 0)
         self.hop(1, 0, 0)
         self.cy = net.send(own, own, net.at(yl=1 - net.yl))
-
-    def step(self, s):
+        self.seen(net.yl, net.z)
+
+    def line(self, line, s):
+        net = self.net
+        yl = net.yl if line == 0 else 1 - net.yl
         if s == 0:
             self.cy.wait_recv()
             self.hop(0, 0, 1)
             self.hop(1, 0, 1)
+            self.seen(yl, net.z)
             return
-        for line in (0, 1):
-            self.up[s - 1, line].wait_recv()
-            if s < 3 or line == 0:
-                self.hop(0, s, line)
-            self.down[s - 1, line].wait_recv()
-            if s < 3 or line == 1:
-                self.hop(1, s, line)
+        self.up[s - 1, line].wait_recv()
+        if s < 3 or line == 0:
+            self.hop(0, s, line)
+        self.down[s - 1, line].wait_recv()
+        if s < 3 or line == 1:
+            self.hop(1, s, line)
+        self.seen(yl, lax.rem(net.z - s + NZ, NZ))
+        self.seen(yl, lax.rem(net.z + s, NZ))
+
+    def own(self, s):
+        self.line(0, s)
+
+    def mate(self, s):
+        self.line(1, s)
 
     def finish(self):
+        net = self.net
+        far = lax.rem(net.z + 4, NZ)
         self.up[3, 0].wait_recv()
+        self.seen(net.yl, far)
         self.down[3, 1].wait_recv()
+        self.seen(1 - net.yl, far)
 
 
 def kernel(
-    slot_ref, p_ref, b_ref, o_ref, m1_ref, m2_ref, r_out, s_out, u_out,
-    prec, tg, gx0, gy0, gy1, gx1,
-    cb, tb, bx0, by0, by1, bx1, bfull,
-    co, to, ox0, oy0, oy1, ox1, ofin, oall,
-    mb, cm, tm, mx0, my0, my1, mx1, mfin,
-    gall, lfull, lacc, stat, smate, dfull, kbuf,
+    slot_ref, a_ref, g_ref, b_ref, o_ref, m1_ref, m2_ref, r_out, s_out, u_out,
+    acts, cot, turned, psend, prec, tg, gx0, gy0, gy1, gx1,
+    cb, tb, bx0, by0, by1, bx1, tc, cx0, cy0, cy1, cx1, bfull, bturn,
+    co, to, ox0, oy0, oy1, ox1, oall,
+    m1, m2, mb, cm, tm, mx0, my0, my1, mx1, mfin,
+    gall, lfull, stat, smate, dfull, kbuf,
     rall, rpick, rmate, sall, spick, sgot,
     usend, urecv, ylsend, ylrecv, ufin, uall,
-    ssem, rsem, asend, arecv,
+    ssem, rsem, asend, arecv, lsem,
 ):
     net = Net(ssem, rsem)
     x, yh, c, yl, z = net.x, net.yh, net.c, net.yl, net.z
@@ -259,103 +281,132 @@
     half_o = pl.ds(pl.multiple_of(c * 32, 32), 32)
     other_o = pl.ds(pl.multiple_of(oc * 32, 32), 32)
 
-    for s in range(2):
-        mb[s, 0:128, :] = m1_ref[s].astype(BF)
-        mb[s, 128:256, :] = m2_ref[s].astype(BF)
-    pl.semaphore_wait(barrier, len(others))
-
-    pcopies = [
-        net.mate(p_ref.at[pl.ds(i * 4, 4), :, other_lanes], prec.at[pl.ds(i * 4, 4)]) for i in range(2)
-    ]
-    bcopy = net.mate(b_ref.at[:, other_b, :], cb.at[pl.ds(2, 2)])
-    ocopy = net.mate(o_ref.at[:, other_o, :], co.at[pl.ds(2, 2)])
-    mcopy = net.mate(mb.at[:, :, other_lanes], cm.at[pl.ds(2, 2)])
-
-    for i in range(2):
-        pcopies[i].wait_recv()
-
-        def add_cores(b, carry):
-            total = p_ref[b, :, half_lanes].astype(F32) + prec[b].astype(F32)
-            tg[b // 2, b % 2] = total.astype(BF)
-            return carry
-
-        lax.fori_loop(i * 4, i * 4 + 4, add_cores, 0)
-    grads = Scatter(net, tg, (gx0, gy0, gy1, gx1), gall.at[yl, z], F32, 32)
-    grads.start()
-
-    for s in range(2):
-        cb[s] = b_ref[s, half_b, :]
-        co[s] = o_ref[s, half_o, :]
-        cm[s] = mb[s, :, half_lanes]
+    def load(i, src, dst):
+        copy = pltpu.make_async_copy(src, dst, lsem.at[i])
+        copy.start()
+        return copy
+
+    load_o = load(0, o_ref.at[:, half_o, :], co.at[pl.ds(0, 2)])
+    load_b = load(1, b_ref.at[:, half_b, :], cb.at[pl.ds(0, 2)])
+    load_a = load(2, a_ref, acts)
+    load_g = load(3, g_ref, cot)
+    load_m = [load(4, m1_ref, m1), load(5, m2_ref, m2)]
     cb[4] = jnp.zeros_like(cb[4])
     co[4] = jnp.zeros_like(co[4])
     cm[4] = jnp.zeros_like(cm[4])
+    pl.semaphore_wait(barrier, len(others))
+
+    ocopy = net.mate(o_ref.at[:, other_o, :], co.at[pl.ds(2, 2)])
+    bcopy = net.mate(b_ref.at[:, other_b, :], cb.at[pl.ds(2, 2)])
+
+    def chooser(chunks, held, first=0):
+        def body(b, carry):
+            chunks[b // 2, b % 2] = held[pick(b), pl.ds(first, chunks.shape[2]), :]
+            return carry
+
+        lax.fori_loop(0, NB, body, 0)
+
+    mine = gall.at[yl, z]
+
+    def statistic(a, b):
+        at = pl.multiple_of((a * NZ + b) * 128, 128)
+        stat[:, pl.ds(at, 128)] = nt(mine[...], gall[a, b])
+
+    right = Scatter(net, to, (ox0, oy0, oy1, ox1), oall.at[yl, z, c], BF, 16)
+    head_b = pl.ds(pl.multiple_of(c * 1024, 128), 384)
+    tail_b = pl.ds(pl.multiple_of(c * 1024 + 384, 128), 640)
+    left = Scatter(net, tb, (bx0, by0, by1, bx1), bfull.at[head_b], BF, 64)
+    rest = Scatter(net, tc, (cx0, cy0, cy1, cx1), bfull.at[tail_b], BF, 64)
+    moments = Scatter(net, tm, (mx0, my0, my1, mx1), mfin, BF, 32)
+    grads = Scatter(net, tg, (gx0, gy0, gy1, gx1), gall.at[yl, z], F32, 32)
+    oring = Ring(net, lambda a, b: oall.at[a, b, c], lambda a, b: None)
+    gring = Ring(net, lambda a, b: gall.at[a, b], statistic)
+
+    load_a.wait()
+    turned[...] = acts[...].T
+    load_o.wait()
+    ocopy.wait_recv()
+    chooser(to, co)
+    right.start()
+    load_g.wait()
+    of_block = lax.broadcasted_iota(jnp.int32, (128, 2048), 1) % NB
+
+    def product(pair, lanes):
+        rows = [
+            jnp.where(of_block == 2 * pair + i, turned[...], jnp.zeros((), BF)) for i in range(2)
+        ]
+        return nn(jnp.concatenate(rows, axis=0), cot[:, lanes]).reshape(2, 128, 512)
+
+    pcopies = []
+    for pair in range(4):
+        psend[pair] = product(pair, other_lanes).astype(BF)
+        pcopies.append(net.mate(psend.at[pair], prec.at[pair]))
+    right.middle()
+    load_b.wait()
     bcopy.wait_recv()
-    ocopy.wait_recv()
+    chooser(tb, cb)
+    left.start()
+    for pair in range(4):
+        own = product(pair, half_lanes)
+        pcopies[pair].wait_recv()
+        tg[pair] = (own + prec[pair].astype(F32)).astype(BF)
+    grads.start()
+
+    right.finish()
+    oring.start()
+    for copy in load_m:
+        copy.wait()
+    for s in range(2):
+        mb[s, 0:128, :] = m1[s].astype(BF)
+        mb[s, 128:256, :] = m2[s].astype(BF)
+    mcopy = net.mate(mb.at[:, :, other_lanes], cm.at[pl.ds(2, 2)])
+    for s in range(2):
+        cm[s] = mb[s, :, half_lanes]
+    chooser(tc, cb, 384)
+    oring.own(1)
     mcopy.wait_recv()
-
-    def choose(b, carry):
-        i = pick(b)
-        tb[b // 2, b % 2] = cb[i]
-        to[b // 2, b % 2] = co[i]
-        tm[b // 2, b % 2] = cm[i]
-        return carry
-
-    lax.fori_loop(0, NB, choose, 0)
+    chooser(tm, cm)
+    oring.own(2)
 
     grads.middle()
-    half16 = pl.ds(pl.multiple_of(c * 8, 8), 8)
-    left = Scatter(net, tb, (bx0, by0, by1, bx1), None, BF, 128)
-    right = Scatter(net, to, (ox0, oy0, oy1, ox1), oall.at[yl, z, c], BF, 16)
-    moments = Scatter(net, tm, (mx0, my0, my1, mx1), mfin, BF, 32)
-    left.out = bfull.at[half_b]
-    left.start()
-    right.start()
+    left.middle()
+    rest.start_x()
+    oring.mate(0)
+    oring.own(3)
     grads.finish()
-
-    gring = Ring(net, lambda a, b: gall.at[a, b])
     gring.start()
-    gring.step(0)
-    gring.step(1)
-    left.middle()
-    gring.step(2)
-    right.middle()
+    rest.start_y()
     moments.start()
-    gring.step(3)
+    oring.mate(1)
+    gring.own(1)
+    gring.mate(0)
     left.finish()
+    gring.own(2)
+    oring.mate(2)
+    gring.mate(1)
+    oring.mate(3)
+    rest.middle()
+    gring.own(3)
+    gring.mate(2)
+    oring.finish()
+    omate = net.mate(oall.at[:, :, c], oall.at[:, :, c])
+    gring.mate(3)
+    moments.middle()
+    rest.finish()
     bmate = net.mate(bfull.at[half_b], bfull.at[half_b])
-    right.finish()
-    oring = Ring(net, lambda a, b: oall.at[a, b, c])
-    oring.start()
-    oring.step(0)
     gring.finish()
     bmate.wait_recv()
-
-    lacc[...] = jnp.zeros_like(lacc)
-    mine = gall.at[yl, z]
-
-    def rows_step(i, carry):
-        part = gall[i // NZ, i % NZ]
-        at = pl.multiple_of(i * 128, 128)
-        lacc[...] += tn(bfull[pl.ds(at, 128), :], part)
-        stat[:, pl.ds(at, 128)] = nt(mine[...], part)
-        return carry
-
-    lax.fori_loop(0, 16, rows_step, 0)
-    lfull[:, half_lanes] = lacc[...].astype(BF)
+    bturn[...] = bfull[...].T
+
+    lfull[:, half_lanes] = nn(bturn[...], gall[...].reshape(2048, 512)).astype(BF)
     lmate = net.mate(lfull.at[:, half_lanes], lfull.at[:, half_lanes])
     mine_s = pl.ds(pl.multiple_of(c * 64, 64), 64)
     other_s = pl.ds(pl.multiple_of(oc * 64, 64), 64)
     cstat = net.mate(stat.at[other_s, :], smate)
-
-    oring.step(1)
-    moments.middle()
-    oring.step(2)
-    oring.step(3)
-    oring.finish()
-    omate = net.mate(oall.at[:, :, c], oall.at[:, :, c])
     cstat.wait_recv()
     sall[x, yh] = (stat[mine_s, :] + smate[...]).astype(BF)
+    sspread = Spread(net, sall)
+    sspread.start()
     lmate.wait_recv()
     omate.wait_recv()
 
@@ -372,9 +423,6 @@
     dmate.wait_recv()
     kbuf[...] = nt(dfull[...], oall[c].reshape(512, 1024)).astype(BF)
 
-    sspread = Spread(net, sall)
-    sspread.start()
-
     def part(zd, yd):
         at = pl.multiple_of((yd * NZ + zd) * 128, 128)
         return nn(bfull[pl.ds(at, 128), :], kbuf[...])
@@ -398,14 +446,6 @@
                 if s > 0 or way == yd:
                     ring_hop(way, s, yd)
 
-    ring_step(0)
-    ring_step(1)
-    rspread.middle()
-    ring_step(2)
-    sspread.middle()
-    ring_step(3)
-
-    rspread.finish()
     zero_r = jnp.zeros((128, 512), BF)
     zero_s = jnp.zeros((64, 2048), BF)
 
@@ -415,6 +455,14 @@
         return jnp.where(b < NB, ref[b0 // 2, b0 % 2], zero)
 
     mate_group = dp - c + oc
+
+    ring_step(0)
+    sspread.middle()
+    ring_step(1)
+    rspread.middle()
+    ring_step(2)
+    ring_step(3)
+    rspread.finish()
     for s in range(2):
         rpick[s] = chosen(rall, zero_r, mate_group, s)
     crm = net.mate(rpick, rmate)
@@ -488,7 +536,7 @@
             ).wait_recv()
 
         value = uall[b]
-        u_out[b] = jnp.where(c == 0, value[:, 0:64], value[:, 64:128])
+        u_out[b] = jnp.where(c == 0, value[:, 0:64], value[:, 64:128]).T
 
     net.drain()
     for j in range(4):
@@ -511,19 +559,27 @@
     ]
 
 
-def step(block_slot, learner, basis_in, basis_out, moment_first, moment_second):
+def step(block_slot, acts, cotangent, basis_in, basis_out, moment_first, moment_second):
     vmem = pl.BlockSpec(memory_space=pltpu.VMEM)
     scratch = (
-        [pltpu.VMEM((8, 128, 512), BF)] + scatter_bufs(128, 512)
-        + [pltpu.VMEM((5, 1024, 128), BF)] + scatter_bufs(1024, 128) + [pltpu.VMEM((2048, 128), BF)]
+        [
+            pltpu.VMEM((2048, 128), BF),
+            pltpu.VMEM((2048, 1024), BF),
+            pltpu.VMEM((128, 2048), BF),
+            pltpu.VMEM((4, 2, 128, 512), BF),
+            pltpu.VMEM((4, 2, 128, 512), BF),
+        ]
+        + scatter_bufs(128, 512)
+        + [pltpu.VMEM((5, 1024, 128), BF)] + scatter_bufs(384, 128) + scatter_bufs(640, 128)
+        + [pltpu.VMEM((2048, 128), BF), pltpu.VMEM((128, 2048), BF)]
         + [pltpu.VMEM((5, 32, 1024), BF)] + scatter_bufs(32, 1024)
-        + [pltpu.VMEM((8, 128), BF), pltpu.VMEM((2, 8, 2, 32, 1024), BF)]
+        + [pltpu.VMEM((2, 8, 2, 32, 1024), BF)]
+        + [pltpu.VMEM((2, 128, 1024), F32), pltpu.VMEM((2, 128, 1024), F32)]
         + [pltpu.VMEM((2, 256, 1024), BF), pltpu.VMEM((5, 256, 512), BF)] + scatter_bufs(256, 512)
         + [pltpu.VMEM((256, 512), BF)]
         + [
             pltpu.VMEM((2, 8, 128, 512), BF),
             pltpu.VMEM((128, 1024), BF),
-            pltpu.VMEM((128, 512), F32),
             pltpu.VMEM((128, 2048), F32),
             pltpu.VMEM((64, 2048), F32),
             pltpu.VMEM((128, 1024), BF),
@@ -544,6 +600,7 @@
             pltpu.SemaphoreType.DMA((128,)),
             pltpu.SemaphoreType.DMA((8,)),
             pltpu.SemaphoreType.DMA((8,)),
+            pltpu.SemaphoreType.DMA((6,)),
         ]
     )
     return pl.pallas_call(
@@ -551,25 +608,32 @@
         out_shape=(
             jax.ShapeDtypeStruct((2, 128, 1024), BF),
             jax.ShapeDtypeStruct((2, 128, 2048), BF),
-            jax.ShapeDtypeStruct((8, 128, 64), BF),
+            jax.ShapeDtypeStruct((8, 64, 128), BF),
         ),
-        in_specs=[pl.BlockSpec(memory_space=pltpu.SMEM)] + [vmem] * 5,
+        in_specs=[pl.BlockSpec(memory_space=pltpu.SMEM)] + [pl.BlockSpec(memory_space=pl.ANY)] * 6,
         out_specs=(vmem, vmem, vmem),
         scratch_shapes=scratch,
         compiler_params=pltpu.CompilerParams(
             collective_id=0, has_side_effects=True, vmem_limit_bytes=56 << 20
         ),
         name="soap_step",
-    )(block_slot, learner, basis_in, basis_out, moment_first, moment_second)
+    )(block_slot, acts, cotangent, basis_in, basis_out, moment_first, moment_second)
 
 
 def per_device(acts, cotangent, block_slot, basis_in, basis_out, moment_first, moment_second):
-    learner = jnp.einsum("tbr,tbo->bro", acts, cotangent, preferred_element_type=F32).astype(BF)
-    rotated, stat, update = step(block_slot, learner, basis_in, basis_out, moment_first, moment_second)
+    rotated, stat, update = step(
+        block_slot,
+        acts.reshape(-1, acts.shape[2]),
+        cotangent.reshape(-1, cotangent.shape[2]),
+        basis_in,
+        basis_out,
+        moment_first,
+        moment_second,
+    )
     rotated = rotated.astype(F32)
     new_first = 0.9 * moment_first + 0.1 * rotated
     new_second = 0.95 * moment_second + 0.05 * rotated * rotated
-    return (new_first, new_second, stat.astype(F32), update)
+    return (new_first, new_second, stat.astype(F32), jnp.swapaxes(update, 1, 2))
 
 
 def solution(mesh):

time: 144 us -> 119 us (0.83)
  Pallas kernels: 129 us -> 113 us
  matrix products: 8.57 us -> 0 us
    pallas_call x1, Pallas kernels: 129 us -> 113 us  [step(): pl.pallas_call(kernel, out_shape=(jax.ShapeDtypeStruct((2, 128, 1024), BF...]
    dot_general x1 -> x0, matrix products: 8.57 us -> none  [per_device(): jnp.einsum('tbr,tbo->bro', acts, cotangent, preferred_element_type=F32)]
where the time goes in v2:
time: 119 us
  Pallas kernels  113 us (95%)
  other arithmetic  4.5 us (4%)
    pallas_call x1, Pallas kernels, step(): pl.pallas_call(kernel, out_shape=(jax.ShapeDtypeStruct((2, 128, 1024), BF...  113 us
    add x1, other arithmetic, per_device(): new_second = 0.95 * moment_second + 0.05 * rotated * rotated  2.94 us

profile of v2, /device:TPU:1, one launch (start us, length us, event | category | flops | bytes accessed | tf_op | source)
XLA Modules:
  0.0 119.2 jit_solution(4160329119288685254)
XLA Ops:
  0.6 0.0 copy-start.1
  0.6 0.0 copy-start
  0.7 113.3 %soap_step.1 = (bf16[2,128,1024]{2,1,0:T(8,128)(2,1)}, bf16[2,128,2048]{2,1,0:T(8,128)(2,1)}, bf16[8,64,128]{2,1,0:T(8,128)(2,1)}) custom-call(s32[8]{0:T(128)} %slot_ref.1, bf16[2048,128]{1,0:T(8,128)(2,1)} %bitcast.4, bf16[2048,1024]{1,0:T(8,128)(2,1)} %bitcast.3, bf16[2,2048,128]{2,1,0:T(8,128)(2,1)} %b_ref.1, bf16[2,64,1024]{2,1,0:T(8,128)(2,1)} %o_ref.1, ...), custom_call_target="tpu_custom_call" | custom-call | tf_op jit(solution)/shard_map/soap_step/pallas_call | solution.py:606
  114.0 0.0 copy-start.2
  114.0 0.0 copy-start.3
  114.0 0.0 copy-done.1
  114.0 0.0 copy-done
  114.0 2.9 %fusion.1 = (f32[2,128,1024]{2,1,0:T(8,128)}, f32[2,128,1024]{2,1,0:T(8,128)}) fusion(bf16[2,128,1024]{2,1,0:T(8,128)(2,1)} %get-tuple-element.7, f32[2,128,1024]{2,1,0:T(8,128)S(1)} %copy-done.1, f32[2,128,1024]{2,1,0:T(8,128)S(1)} %copy-done), kind=kLoop, calls=%fused_computation.3 | loop fusion | flops 2097152 | bytes 4718592 | tf_op jit(solution)/shard_map/add | solution.py:635
  117.0 0.0 copy-done.2
  117.0 1.6 %convert_element_type.7 = f32[2,128,2048]{2,1,0:T(8,128)} convert(bf16[2,128,2048]{2,1,0:T(8,128)(2,1)S(1)} %copy-done.2) | non-fusion elementwise | flops 524288 | bytes 3145728 | tf_op jit(solution)/shard_map/convert_element_type | solution.py:636
  118.5 0.0 copy-done.3
  118.5 0.7 copy.12
Async XLA Ops:
  0.6 113.4 %copy-start.1 = (f32[2,128,1024]{2,1,0:T(8,128)S(1)}, f32[2,128,1024]{2,1,0:T(8,128)}, u32[]{:S(2)}) copy-start(f32[2,128,1024]{2,1,0:T(8,128)} %m2_ref.1) | copy-start | bytes 3145732
  0.6 113.4 %copy-start = (f32[2,128,1024]{2,1,0:T(8,128)S(1)}, f32[2,128,1024]{2,1,0:T(8,128)}, u32[]{:S(2)}) copy-start(f32[2,128,1024]{2,1,0:T(8,128)} %m1_ref.1) | copy-start | bytes 3145732
  114.0 3.0 %copy-start.2 = (bf16[2,128,2048]{2,1,0:T(8,128)(2,1)S(1)}, bf16[2,128,2048]{2,1,0:T(8,128)(2,1)}, u32[]{:S(2)}) copy-start(bf16[2,128,2048]{2,1,0:T(8,128)(2,1)} %get-tuple-element.8) | copy-start | bytes 3145732
  114.0 4.5 %copy-start.3 = (bf16[8,64,128]{2,1,0:T(8,128)(2,1)S(1)}, bf16[8,64,128]{2,1,0:T(8,128)(2,1)}, u32[]{:S(2)}) copy-start(bf16[8,64,128]{2,1,0:T(8,128)(2,1)} %get-tuple-element.9) | copy-start | bytes 393220

commit v3 on v2

--- a/solution.py
+++ b/solution.py
@@ -71,8 +71,8 @@
     def __init__(self, net, t, bufs, out, kind, step):
         self.net, self.t, self.out, self.kind, self.step = net, t, out, kind, step
         self.x0, self.y0, self.y1, self.x1 = bufs
-        self.rows = t.shape[2]
-        self.half = self.rows // 2
+        self.half = self.y0.shape[0]
+        self.left = t.shape[2] - self.half
 
     def start_x(self):
         net, h = self.net, self.half
@@ -84,15 +84,14 @@
     def start_y(self):
         net, h = self.net, self.half
         self.cy1 = net.send(
-            self.t.at[:, 1 - net.yh, pl.ds(h, h), :], self.y1, net.at(yh=1 - net.yh)
+            self.t.at[:, 1 - net.yh, pl.ds(h, self.left), :], self.y1, net.at(yh=1 - net.yh)
         )
 
     def start(self):
         self.start_y()
         self.start_x()
 
-    def add(self, dst, srcs):
-        total = None
+    def add(self, dst, srcs, count):
         n, kind = self.step, self.kind
 
         def body(i, carry):
@@ -104,8 +103,7 @@
             dst(rows, total.astype(BF))
             return carry
 
-        del total
-        lax.fori_loop(0, self.half // n, body, 0)
+        lax.fori_loop(0, count // n, body, 0)
 
     def rows_of(self, ref, base=0):
         def load(rows):
@@ -128,6 +126,7 @@
             self.add(
                 self.store_of(mine),
                 [self.rows_of(mine)] + [self.rows_of(self.x0.at[k, yp]) for k in range(3)],
+                h,
             )
             if yp is not net.yh:
                 self.cy0 = net.send(
@@ -137,22 +136,27 @@
         self.cx1 = []
         for k, xp in enumerate(net.xs() + [net.x]):
             mine = t.at[xp, net.yh]
-            self.add(self.store_of(mine, h), [self.rows_of(mine, h), self.rows_of(self.y1.at[xp])])
+            self.add(
+                self.store_of(mine, h),
+                [self.rows_of(mine, h), self.rows_of(self.y1.at[xp])],
+                self.left,
+            )
             if k < 3:
                 self.cx1.append(
-                    net.send(t.at[xp, net.yh, pl.ds(h, h), :], self.x1.at[k], net.at(x=xp))
+                    net.send(t.at[xp, net.yh, pl.ds(h, self.left), :], self.x1.at[k], net.at(x=xp))
                 )
 
     def finish(self):
         net, h = self.net, self.half
         mine = self.t.at[net.x, net.yh]
         self.cy0.wait_recv()
-        self.add(self.store_of(self.out), [self.rows_of(mine), self.rows_of(self.y0)])
+        self.add(self.store_of(self.out), [self.rows_of(mine), self.rows_of(self.y0)], h)
         for copy in self.cx1:
             copy.wait_recv()
         self.add(
             self.store_of(self.out, h),
             [self.rows_of(mine, h)] + [self.rows_of(self.x1.at[k]) for k in range(3)],
+            self.left,
         )
 
 
@@ -184,43 +188,48 @@
 
 
 class Ring:
-    def __init__(self, net, block, seen):
-        self.net, self.block, self.seen = net, block, seen
+    def __init__(self, net, block, parts, seen):
+        self.net, self.block, self.parts, self.seen = net, block, range(parts), seen
         self.up, self.down = {}, {}
 
-    def hop(self, way, step, line):
+    def hop(self, way, step, line, p):
         net = self.net
         yl = net.yl if line == 0 else 1 - net.yl
         sign = 1 if way == 0 else -1
-        ref = self.block(yl, lax.rem(net.z - sign * step + NZ, NZ))
+        ref = self.block(yl, lax.rem(net.z - sign * step + NZ, NZ), p)
         copy = net.send(ref, ref, net.at(z=lax.rem(net.z + sign + NZ, NZ)))
-        (self.up if way == 0 else self.down)[step, line] = copy
+        (self.up if way == 0 else self.down)[step, line, p] = copy
 
     def start(self):
         net = self.net
-        own = self.block(net.yl, net.z)
-        self.hop(0, 0, 0)
-        self.hop(1, 0, 0)
-        self.cy = net.send(own, own, net.at(yl=1 - net.yl))
+        self.cy = []
+        for p in self.parts:
+            own = self.block(net.yl, net.z, p)
+            self.hop(0, 0, 0, p)
+            self.hop(1, 0, 0, p)
+            self.cy.append(net.send(own, own, net.at(yl=1 - net.yl)))
         self.seen(net.yl, net.z)
 
     def line(self, line, s):
         net = self.net
         yl = net.yl if line == 0 else 1 - net.yl
+        for p in self.parts:
+            if s == 0:
+                self.cy[p].wait_recv()
+                self.hop(0, 0, 1, p)
+                self.hop(1, 0, 1, p)
+                continue
+            self.up[s - 1, line, p].wait_recv()
+            if s < 3 or line == 0:
+                self.hop(0, s, line, p)
+            self.down[s - 1, line, p].wait_recv()
+            if s < 3 or line == 1:
+                self.hop(1, s, line, p)
         if s == 0:
-            self.cy.wait_recv()
-            self.hop(0, 0, 1)
-            self.hop(1, 0, 1)
             self.seen(yl, net.z)
-            return
-        self.up[s - 1, line].wait_recv()
-        if s < 3 or line == 0:
-            self.hop(0, s, line)
-        self.down[s - 1, line].wait_recv()
-        if s < 3 or line == 1:
-            self.hop(1, s, line)
-        self.seen(yl, lax.rem(net.z - s + NZ, NZ))
-        self.seen(yl, lax.rem(net.z + s, NZ))
+        else:
+            self.seen(yl, lax.rem(net.z - s + NZ, NZ))
+            self.seen(yl, lax.rem(net.z + s, NZ))
 
     def own(self, s):
         self.line(0, s)
@@ -231,9 +240,11 @@
     def finish(self):
         net = self.net
         far = lax.rem(net.z + 4, NZ)
-        self.up[3, 0].wait_recv()
+        for p in self.parts:
+            self.up[3, 0, p].wait_recv()
         self.seen(net.yl, far)
-        self.down[3, 1].wait_recv()
+        for p in self.parts:
+            self.down[3, 1, p].wait_recv()
         self.seen(1 - net.yl, far)
 
 
@@ -319,8 +330,8 @@
     rest = Scatter(net, tc, (cx0, cy0, cy1, cx1), bfull.at[tail_b], BF, 64)
     moments = Scatter(net, tm, (mx0, my0, my1, mx1), mfin, BF, 32)
     grads = Scatter(net, tg, (gx0, gy0, gy1, gx1), gall.at[yl, z], F32, 32)
-    oring = Ring(net, lambda a, b: oall.at[a, b, c], lambda a, b: None)
-    gring = Ring(net, lambda a, b: gall.at[a, b], statistic)
+    oring = Ring(net, lambda a, b, p: oall.at[a, b, c], 1, lambda a, b: None)
+    gring = Ring(net, lambda a, b, p: gall.at[a, b, pl.ds(p * 64, 64), :], 2, statistic)
 
     load_a.wait()
     turned[...] = acts[...].T
@@ -328,6 +339,10 @@
     ocopy.wait_recv()
     chooser(to, co)
     right.start()
+    load_b.wait()
+    bcopy.wait_recv()
+    chooser(tb, cb)
+    left.start()
     load_g.wait()
     of_block = lax.broadcasted_iota(jnp.int32, (128, 2048), 1) % NB
 
@@ -341,15 +356,12 @@
     for pair in range(4):
         psend[pair] = product(pair, other_lanes).astype(BF)
         pcopies.append(net.mate(psend.at[pair], prec.at[pair]))
-    right.middle()
-    load_b.wait()
-    bcopy.wait_recv()
-    chooser(tb, cb)
-    left.start()
     for pair in range(4):
         own = product(pair, half_lanes)
         pcopies[pair].wait_recv()
         tg[pair] = (own + prec[pair].astype(F32)).astype(BF)
+        if pair == 1:
+            right.middle()
     grads.start()
 
     right.finish()
@@ -375,18 +387,19 @@
     oring.own(3)
     grads.finish()
     gring.start()
-    rest.start_y()
-    moments.start()
+    moments.start_x()
     oring.mate(1)
     gring.own(1)
     gring.mate(0)
+    rest.start_y()
+    moments.start_y()
     left.finish()
     gring.own(2)
     oring.mate(2)
     gring.mate(1)
     oring.mate(3)
+    gring.own(3)
     rest.middle()
-    gring.own(3)
     gring.mate(2)
     oring.finish()
     omate = net.mate(oall.at[:, :, c], oall.at[:, :, c])
@@ -423,28 +436,26 @@
     dmate.wait_recv()
     kbuf[...] = nt(dfull[...], oall[c].reshape(512, 1024)).astype(BF)
 
-    def part(zd, yd):
-        at = pl.multiple_of((yd * NZ + zd) * 128, 128)
-        return nn(bfull[pl.ds(at, 128), :], kbuf[...])
+    def part(zd, yd, p):
+        at = pl.multiple_of((yd * NZ + zd) * 128 + p * 64, 64)
+        return nn(bfull[pl.ds(at, 64), :], kbuf[...])
 
     hops = {}
-
-    def ring_hop(way, s, yd):
+    lines = (1 - yl, yl)
+
+    def ring_hop(way, line, s):
         sign = 1 if way == 0 else -1
-        value = part(lax.rem(z + sign * (4 - s) + NZ, NZ), yd)
-        if (way, s - 1, yd) in hops:
-            hops[way, s - 1, yd].wait_recv()
-            value = value + urecv[way, s - 1, yd].astype(F32)
-        usend[way, s, yd] = value.astype(BF)
-        hops[way, s, yd] = net.send(
-            usend.at[way, s, yd], urecv.at[way, s, yd], net.at(z=lax.rem(z + sign + NZ, NZ))
-        )
-
-    def ring_step(s):
-        for yd in (0, 1):
-            for way in (0, 1):
-                if s > 0 or way == yd:
-                    ring_hop(way, s, yd)
+        for p in range(2):
+            value = part(lax.rem(z + sign * (4 - s) + NZ, NZ), lines[line], p)
+            if (way, line, s - 1, p) in hops:
+                hops[way, line, s - 1, p].wait_recv()
+                value = value + urecv[way, s - 1, line, p].astype(F32)
+            usend[way, s, line, p] = value.astype(BF)
+            hops[way, line, s, p] = net.send(
+                usend.at[way, s, line, p],
+                urecv.at[way, s, line, p],
+                net.at(z=lax.rem(z + sign + NZ, NZ)),
+            )
 
     zero_r = jnp.zeros((128, 512), BF)
     zero_s = jnp.zeros((64, 2048), BF)
@@ -456,33 +467,45 @@
 
     mate_group = dp - c + oc
 
-    ring_step(0)
+    ring_hop(0, 0, 0)
+    ring_hop(1, 1, 0)
+    ring_hop(0, 1, 1)
+    ring_hop(1, 0, 1)
     sspread.middle()
-    ring_step(1)
+    ring_hop(0, 0, 1)
+    ring_hop(1, 1, 1)
+    ring_hop(0, 1, 2)
+    ring_hop(1, 0, 2)
     rspread.middle()
-    ring_step(2)
-    ring_step(3)
+    ring_hop(0, 0, 2)
+    ring_hop(1, 1, 2)
+    ring_hop(1, 0, 3)
+    ring_hop(0, 0, 3)
+    ring_hop(0, 1, 3)
+    ring_hop(1, 1, 3)
     rspread.finish()
     for s in range(2):
         rpick[s] = chosen(rall, zero_r, mate_group, s)
     crm = net.mate(rpick, rmate)
 
-    for way in (0, 1):
-        for yd in (0, 1):
-            hops[way, 3, yd].wait_recv()
-
-    def final(yd):
-        return part(z, yd) + urecv[0, 3, yd].astype(F32) + urecv[1, 3, yd].astype(F32)
-
-    ylsend[...] = final(1 - yl).astype(BF)
-    cyl = net.send(ylsend, ylrecv, net.at(yl=1 - yl))
-    own = final(yl)
+    def final(line, p):
+        for way in (0, 1):
+            hops[way, line, 3, p].wait_recv()
+        here = part(z, lines[line], p)
+        return here + urecv[0, 3, line, p].astype(F32) + urecv[1, 3, line, p].astype(F32)
+
+    cyl = []
+    for p in range(2):
+        ylsend[p] = final(0, p).astype(BF)
+        cyl.append(net.send(ylsend.at[p], ylrecv.at[p], net.at(yl=1 - yl)))
     sspread.finish()
     for s in range(2):
         spick[s] = chosen(sall, zero_s, mate_group, s)
     csm = net.mate(spick, sgot)
-    cyl.wait_recv()
-    ufin[...] = (own + ylrecv[...].astype(F32)).astype(BF)
+    for p in range(2):
+        own = final(1, p)
+        cyl[p].wait_recv()
+        ufin[p * 64 : (p + 1) * 64, :] = (own + ylrecv[p].astype(F32)).astype(BF)
 
     def to_columns(j, k):
         tx, ty = 2 * c + j // 2, j % 2
@@ -548,14 +571,14 @@
                 copy().wait_send()
 
 
-def scatter_bufs(rows, lanes):
-    h = rows // 2
+def scatter_bufs(rows, lanes, h=None):
+    h = rows // 2 if h is None else h
     return [
         pltpu.VMEM((4, 2, rows, lanes), BF),
         pltpu.VMEM((3, 2, h, lanes), BF),
         pltpu.VMEM((h, lanes), BF),
-        pltpu.VMEM((4, h, lanes), BF),
-        pltpu.VMEM((3, h, lanes), BF),
+        pltpu.VMEM((4, rows - h, lanes), BF),
+        pltpu.VMEM((3, rows - h, lanes), BF),
     ]
 
 
@@ -575,7 +598,7 @@
         + [pltpu.VMEM((5, 32, 1024), BF)] + scatter_bufs(32, 1024)
         + [pltpu.VMEM((2, 8, 2, 32, 1024), BF)]
         + [pltpu.VMEM((2, 128, 1024), F32), pltpu.VMEM((2, 128, 1024), F32)]
-        + [pltpu.VMEM((2, 256, 1024), BF), pltpu.VMEM((5, 256, 512), BF)] + scatter_bufs(256, 512)
+        + [pltpu.VMEM((2, 256, 1024), BF), pltpu.VMEM((5, 256, 512), BF)] + scatter_bufs(256, 512, 160)
         + [pltpu.VMEM((256, 512), BF)]
         + [
             pltpu.VMEM((2, 8, 128, 512), BF),
@@ -590,14 +613,14 @@
             pltpu.VMEM((4, 2, 64, 2048), BF),
             pltpu.VMEM((2, 64, 2048), BF),
             pltpu.VMEM((2, 64, 2048), BF),
-            pltpu.VMEM((2, 4, 2, 128, 512), BF),
-            pltpu.VMEM((2, 4, 2, 128, 512), BF),
-            pltpu.VMEM((128, 512), BF),
-            pltpu.VMEM((128, 512), BF),
+            pltpu.VMEM((2, 4, 2, 2, 64, 512), BF),
+            pltpu.VMEM((2, 4, 2, 2, 64, 512), BF),
+            pltpu.VMEM((2, 64, 512), BF),
+            pltpu.VMEM((2, 64, 512), BF),
             pltpu.VMEM((128, 512), BF),
             pltpu.VMEM((8, 128, 128), BF),
-            pltpu.SemaphoreType.DMA((128,)),
-            pltpu.SemaphoreType.DMA((128,)),
+            pltpu.SemaphoreType.DMA((192,)),
+            pltpu.SemaphoreType.DMA((192,)),
             pltpu.SemaphoreType.DMA((8,)),
             pltpu.SemaphoreType.DMA((8,)),
             pltpu.SemaphoreType.DMA((6,)),

time: 119 us -> 118 us (level)
    pallas_call x1, Pallas kernels: 113 us -> 112 us  [step(): pl.pallas_call(kernel, out_shape=(jax.ShapeDtypeStruct((2, 128, 1024), BF...]
where the time goes in v3:
time: 118 us
  Pallas kernels  112 us (95%)
  other arithmetic  4.5 us (4%)
    pallas_call x1, Pallas kernels, step(): pl.pallas_call(kernel, out_shape=(jax.ShapeDtypeStruct((2, 128, 1024), BF...  112 us
    add x1, other arithmetic, per_device(): new_second = 0.95 * moment_second + 0.05 * rotated * rotated  2.94 us

profile of v3, /device:TPU:1, one launch (start us, length us, event | category | flops | bytes accessed | tf_op | source)
XLA Modules:
  0.0 118.0 jit_solution(5252161761820497913)
XLA Ops:
  0.6 0.0 copy-start.1
  0.6 0.0 copy-start
  0.7 112.1 %soap_step.1 = (bf16[2,128,1024]{2,1,0:T(8,128)(2,1)}, bf16[2,128,2048]{2,1,0:T(8,128)(2,1)}, bf16[8,64,128]{2,1,0:T(8,128)(2,1)}) custom-call(s32[8]{0:T(128)} %slot_ref.1, bf16[2048,128]{1,0:T(8,128)(2,1)} %bitcast.4, bf16[2048,1024]{1,0:T(8,128)(2,1)} %bitcast.3, bf16[2,2048,128]{2,1,0:T(8,128)(2,1)} %b_ref.1, bf16[2,64,1024]{2,1,0:T(8,128)(2,1)} %o_ref.1, ...), custom_call_target="tpu_custom_call" | custom-call | tf_op jit(solution)/shard_map/soap_step/pallas_call | solution.py:629
  112.8 0.0 copy-start.2
  112.8 0.0 copy-start.3
  112.8 0.0 copy-done.1
  112.8 0.0 copy-done
  112.8 2.9 %fusion.1 = (f32[2,128,1024]{2,1,0:T(8,128)}, f32[2,128,1024]{2,1,0:T(8,128)}) fusion(bf16[2,128,1024]{2,1,0:T(8,128)(2,1)} %get-tuple-element.7, f32[2,128,1024]{2,1,0:T(8,128)S(1)} %copy-done.1, f32[2,128,1024]{2,1,0:T(8,128)S(1)} %copy-done), kind=kLoop, calls=%fused_computation.3 | loop fusion | flops 2097152 | bytes 4718592 | tf_op jit(solution)/shard_map/add | solution.py:658
  115.8 0.0 copy-done.2
  115.8 1.6 %convert_element_type.7 = f32[2,128,2048]{2,1,0:T(8,128)} convert(bf16[2,128,2048]{2,1,0:T(8,128)(2,1)S(1)} %copy-done.2) | non-fusion elementwise | flops 524288 | bytes 3145728 | tf_op jit(solution)/shard_map/convert_element_type | solution.py:659
  117.3 0.0 copy-done.3
  117.3 0.7 copy.12
Async XLA Ops:
  0.6 112.2 %copy-start.1 = (f32[2,128,1024]{2,1,0:T(8,128)S(1)}, f32[2,128,1024]{2,1,0:T(8,128)}, u32[]{:S(2)}) copy-start(f32[2,128,1024]{2,1,0:T(8,128)} %m2_ref.1) | copy-start | bytes 3145732
  0.6 112.2 %copy-start = (f32[2,128,1024]{2,1,0:T(8,128)S(1)}, f32[2,128,1024]{2,1,0:T(8,128)}, u32[]{:S(2)}) copy-start(f32[2,128,1024]{2,1,0:T(8,128)} %m1_ref.1) | copy-start | bytes 3145732
  112.8 3.0 %copy-start.2 = (bf16[2,128,2048]{2,1,0:T(8,128)(2,1)S(1)}, bf16[2,128,2048]{2,1,0:T(8,128)(2,1)}, u32[]{:S(2)}) copy-start(bf16[2,128,2048]{2,1,0:T(8,128)(2,1)} %get-tuple-element.8) | copy-start | bytes 3145732
  112.8 4.5 %copy-start.3 = (bf16[8,64,128]{2,1,0:T(8,128)(2,1)S(1)}, bf16[8,64,128]{2,1,0:T(8,128)(2,1)}, u32[]{:S(2)}) copy-start(bf16[8,64,128]{2,1,0:T(8,128)(2,1)} %get-tuple-element.9) | copy-start | bytes 393220

commit v4 on v3

--- a/solution.py
+++ b/solution.py
@@ -407,15 +407,15 @@
     moments.middle()
     rest.finish()
     bmate = net.mate(bfull.at[half_b], bfull.at[half_b])
-    gring.finish()
     bmate.wait_recv()
     bturn[...] = bfull[...].T
-
-    lfull[:, half_lanes] = nn(bturn[...], gall[...].reshape(2048, 512)).astype(BF)
-    lmate = net.mate(lfull.at[:, half_lanes], lfull.at[:, half_lanes])
+    gring.finish()
     mine_s = pl.ds(pl.multiple_of(c * 64, 64), 64)
     other_s = pl.ds(pl.multiple_of(oc * 64, 64), 64)
     cstat = net.mate(stat.at[other_s, :], smate)
+
+    lfull[:, half_lanes] = nn(bturn[...], gall[...].reshape(2048, 512)).astype(BF)
+    lmate = net.mate(lfull.at[:, half_lanes], lfull.at[:, half_lanes])
     cstat.wait_recv()
     sall[x, yh] = (stat[mine_s, :] + smate[...]).astype(BF)
     sspread = Spread(net, sall)

time: 118 us -> 117 us (level)
  no operation moved by 1% of the time
where the time goes in v4:
time: 117 us
  Pallas kernels  111 us (95%)
  other arithmetic  4.5 us (4%)
    pallas_call x1, Pallas kernels, step(): pl.pallas_call(kernel, out_shape=(jax.ShapeDtypeStruct((2, 128, 1024), BF...  111 us
    add x1, other arithmetic, per_device(): new_second = 0.95 * moment_second + 0.05 * rotated * rotated  2.94 us

profile of v4, /device:TPU:1, one launch (start us, length us, event | category | flops | bytes accessed | tf_op | source)
XLA Modules:
  0.0 116.8 jit_solution(6355165707479500309)
XLA Ops:
  0.6 0.0 copy-start.1
  0.6 0.0 copy-start
  0.7 111.0 %soap_step.1 = (bf16[2,128,1024]{2,1,0:T(8,128)(2,1)}, bf16[2,128,2048]{2,1,0:T(8,128)(2,1)}, bf16[8,64,128]{2,1,0:T(8,128)(2,1)}) custom-call(s32[8]{0:T(128)} %slot_ref.1, bf16[2048,128]{1,0:T(8,128)(2,1)} %bitcast.4, bf16[2048,1024]{1,0:T(8,128)(2,1)} %bitcast.3, bf16[2,2048,128]{2,1,0:T(8,128)(2,1)} %b_ref.1, bf16[2,64,1024]{2,1,0:T(8,128)(2,1)} %o_ref.1, ...), custom_call_target="tpu_custom_call" | custom-call | tf_op jit(solution)/shard_map/soap_step/pallas_call | solution.py:629
  111.7 0.0 copy-start.2
  111.7 0.0 copy-start.3
  111.7 0.0 copy-done.1
  111.7 0.0 copy-done
  111.7 2.9 %fusion.1 = (f32[2,128,1024]{2,1,0:T(8,128)}, f32[2,128,1024]{2,1,0:T(8,128)}) fusion(bf16[2,128,1024]{2,1,0:T(8,128)(2,1)} %get-tuple-element.7, f32[2,128,1024]{2,1,0:T(8,128)S(1)} %copy-done.1, f32[2,128,1024]{2,1,0:T(8,128)S(1)} %copy-done), kind=kLoop, calls=%fused_computation.3 | loop fusion | flops 2097152 | bytes 4718592 | tf_op jit(solution)/shard_map/add | solution.py:658
  114.6 0.0 copy-done.2
  114.6 1.6 %convert_element_type.7 = f32[2,128,2048]{2,1,0:T(8,128)} convert(bf16[2,128,2048]{2,1,0:T(8,128)(2,1)S(1)} %copy-done.2) | non-fusion elementwise | flops 524288 | bytes 3145728 | tf_op jit(solution)/shard_map/convert_element_type | solution.py:659
  116.2 0.0 copy-done.3
  116.2 0.7 copy.12
Async XLA Ops:
  0.6 111.0 %copy-start.1 = (f32[2,128,1024]{2,1,0:T(8,128)S(1)}, f32[2,128,1024]{2,1,0:T(8,128)}, u32[]{:S(2)}) copy-start(f32[2,128,1024]{2,1,0:T(8,128)} %m2_ref.1) | copy-start | bytes 3145732
  0.6 111.0 %copy-start = (f32[2,128,1024]{2,1,0:T(8,128)S(1)}, f32[2,128,1024]{2,1,0:T(8,128)}, u32[]{:S(2)}) copy-start(f32[2,128,1024]{2,1,0:T(8,128)} %m1_ref.1) | copy-start | bytes 3145732
  111.7 3.0 %copy-start.2 = (bf16[2,128,2048]{2,1,0:T(8,128)(2,1)S(1)}, bf16[2,128,2048]{2,1,0:T(8,128)(2,1)}, u32[]{:S(2)}) copy-start(bf16[2,128,2048]{2,1,0:T(8,128)(2,1)} %get-tuple-element.8) | copy-start | bytes 3145732
  111.7 4.5 %copy-start.3 = (bf16[8,64,128]{2,1,0:T(8,128)(2,1)S(1)}, bf16[8,64,128]{2,1,0:T(8,128)(2,1)}, u32[]{:S(2)}) copy-start(bf16[8,64,128]{2,1,0:T(8,128)(2,1)} %get-tuple-element.9) | copy-start | bytes 393220
